TPU v7x, 1024 devices: a whole 4x8x16 slice. The times are simulated.
1024 devices in a mesh: pair: 8 (over y), contr: 128 (over x, z, core).
Axes of the slice: x: 4, y: 8, z: 16, core: 2. Of those that a mesh axis runs over, the one named last changes fastest.
Arguments:
- amplitudes: bfloat16 [4096, 131072], P('pair', 'contr'), may hold values from -24 to 24
- integrals: bfloat16 [131072, 1024], P('contr', 'pair'), may hold values from -0.046875 to 0.046875
- occ_irrep: int32 [256], replicated, may hold values from 0 to 7
- virt_irrep: int32 [512], replicated, may hold values from 0 to 7
- occ_energy: float32 [256], replicated, may hold values from -2 to -0.5
- virt_energy: float32 [512], replicated, may hold values from 0.5 to 3
- slab_start: int32 [2], replicated, may hold values from 0 to 496
Outputs:
- update: bfloat16 [4096, 1024], P(('pair', 'contr'))
All inputs are finite; a program needn't handle non-finite values.
Results may differ from a plain program's by a relative error of at most 0.003.
Values may be sent and summed in bfloat16 or wider, within the bound.
A program may use at most 64 MiB of HBM per device.

v0:
```python
import jax
import jax.numpy as jnp
from jax import lax
from jax.sharding import PartitionSpec as P


def body(amplitudes, integrals, occ_irrep, virt_irrep, occ_energy, virt_energy, slab_start):
    pair_count = lax.axis_size("pair")
    contr_count = lax.axis_size("contr")
    pair_index = lax.axis_index("pair")
    contr_index = lax.axis_index("contr")
    virt_count = virt_irrep.shape[0]
    kc_local = integrals.shape[0]
    occ_local = kc_local // virt_count
    rows_pair = amplitudes.shape[0]
    cols_pair = integrals.shape[1]
    rows_device = rows_pair // contr_count
    slab_first = amplitudes.shape[0] * pair_count // occ_irrep.shape[0]
    slab_second = cols_pair * pair_count // occ_irrep.shape[0]
    first_start = slab_start[0]
    second_start = slab_start[1]
    a_irrep = lax.dynamic_slice(virt_irrep, (first_start,), (slab_first,))
    b_irrep = lax.dynamic_slice(virt_irrep, (second_start,), (slab_second,))
    a_energy = lax.dynamic_slice(virt_energy, (first_start,), (slab_first,))
    b_energy = lax.dynamic_slice(virt_energy, (second_start,), (slab_second,))
    row_irrep = jnp.bitwise_xor(occ_irrep[:, None], a_irrep[None, :]).reshape(-1)
    col_irrep = jnp.bitwise_xor(occ_irrep[:, None], b_irrep[None, :]).reshape(-1)
    row_energy = (occ_energy[:, None] - a_energy[None, :]).reshape(-1)
    col_energy = (occ_energy[:, None] - b_energy[None, :]).reshape(-1)
    local_occ = lax.dynamic_slice(occ_irrep, (contr_index * occ_local,), (occ_local,))
    kc_irrep = jnp.bitwise_xor(local_occ[:, None], virt_irrep[None, :]).reshape(-1)
    zero = jnp.zeros((), jnp.bfloat16)
    whole_int = lax.all_gather(integrals, "pair", axis=1, tiled=True)
    int_masked = jnp.where(kc_irrep[:, None] == col_irrep[None, :], whole_int, zero)
    row_irrep_pair = lax.dynamic_slice(row_irrep, (pair_index * rows_pair,), (rows_pair,))
    amp_masked = jnp.where(row_irrep_pair[:, None] == kc_irrep[None, :], amplitudes, zero)
    summed = lax.psum_scatter(
        jnp.dot(amp_masked, int_masked, preferred_element_type=jnp.float32),
        "contr",
        scatter_dimension=0,
        tiled=True,
    )
    mine_energy = lax.dynamic_slice(
        row_energy, (pair_index * rows_pair + contr_index * rows_device,), (rows_device,)
    )
    update = (summed / (mine_energy[:, None] + col_energy[None, :])).astype(jnp.bfloat16)
    return update


def solution(mesh):
    in_specs = (P("pair", "contr"), P("contr", "pair"), P(), P(), P(), P(), P())
    out_specs = P(("pair", "contr"), None)
    return jax.shard_map(body, mesh=mesh, in_specs=in_specs, out_specs=out_specs, check_vma=False)
```

profile of v0, /device:TPU:1, one launch (start us, length us, event | category | flops | bytes accessed | tf_op | source)
XLA Modules:
  0.0 447.6 jit_solution(12400257481825537240)
XLA Ops:
  6.5 0.0 all-gather.2.cloned.1.call-start
  6.5 0.7 all-gather.2.cloned.1.call-update
  7.3 0.0 all-reduce.3.cloned.1.call-start
  7.3 1.4 fusion.9
  12.0 0.8 dynamic_slice.21
  12.8 0.8 broadcast_xor_fusion.1
  13.5 0.1 xor.64
  13.6 0.8 dynamic_slice.23
  14.4 0.8 xor_bitcast_fusion
  15.8 0.8 dynamic_slice.24
  16.6 0.8 broadcast_xor_fusion
  17.4 0.1 xor.72
  17.5 0.1 dynamic_slice.22
  17.6 52.3 %all-gather.2.cloned.1.call-done = bf16[1024,1024]{1,0:T(8,128)(2,1)} async-done(((bf16[1024,128]{1,0:T(8,128)(2,1)}), bf16[1024,1024]{1,0:T(8,128)(2,1)}) %all-gather.2.cloned.1.call-update) | async-done | bytes 2097168 | tf_op jit(solution)/shard_map/all_gather | solution.py:33
  69.9 4.7 %fusion = f32[512,1024]{1,0:T(8,128)} fusion(bf16[1024,1024]{1,0:T(8,128)(2,1)} %all-gather.2.cloned.1.call-done, s32[1024]{0:T(1024)S(1)} %xor.72, s32[1024]{0:T(1024)S(1)} %bitcast.6, bf16[512,1024]{1,0:T(8,128)(2,1)} %param.7, s32[512]{0:T(512)S(1)} %dynamic_slice.22), kind=kOutput, calls=%fused_computation.1 | convolution fusion | flops 1076887552 | bytes 5253120 | tf_op jit(solution)/shard_map/dot_general | solution.py:38
  74.6 0.0 copy-start.1
  74.6 0.0 copy-start
  74.6 0.0 all-reduce.3.cloned.1.call-update
  74.7 0.6 copy-done.1
  75.3 0.1 dynamic_slice.25
  75.4 0.1 dynamic_slice.27
  75.5 0.0 copy-done
  75.5 0.1 broadcast_subtract_fusion.1
  75.6 0.1 sub.40
  75.7 0.1 broadcast_subtract_fusion
  75.8 0.1 sub.44
  75.9 0.1 dynamic_slice.26
  76.0 1.3 dynamic-slice
  77.9 361.5 %all-reduce.3.cloned.1.call-done = f32[512,1024]{1,0:T(8,128)} async-done(((f32[512,1024]{1,0:T(8,128)}), f32[512,1024]{1,0:T(8,128)}) %all-reduce.3.cloned.1.call-update) | async-done | bytes 2097168
  439.4 1.4 fusion.7
  (1 shorter events, 0.0 us)
Async XLA Ops:
  6.5 63.4 %all-gather.2.cloned.1.call-start = ((), (), s32[]{:S(2)}) async-start(), calls=%async_computation | async-start | bytes 2359296 | tf_op jit(solution)/shard_map/all_gather | solution.py:33
  7.3 432.1 %all-reduce.3.cloned.1.call-start = ((), (), s32[]{:S(2)}) async-start(), calls=%async_computation.1 | async-start | bytes 4194304
  74.6 0.7 copy-start.1
  74.6 0.8 copy-start
Sparse Core Ops, SparseCore 0:
  9.9 59.9 all-gather.1
  74.8 364.5 all-reduce.2
where the time goes:
time: 448 us
  waiting for transfers between devices  415 us (93%)
  between operations  18.1 us (4%)
  local copies, waits for them, and re-layouts  6.31 us (1%)
  matrix products  4.71 us (1%)
    unnamed x3, waiting for transfers between devices  362 us
    all_gather x1, waiting for transfers between devices, body(): whole_int = lax.all_gather(integrals, 'pair', axis=1, tiled=True)  52.3 us
  transfers between devices with their start and end apart: 2, of which 2 were waited for; matrix products, arithmetic and copies ran while one was open for 2% of the time, Pallas kernels for 0%

commit v1 on v0

--- a/solution.py
+++ b/solution.py
@@ -1,10 +1,389 @@
+import functools
+
 import jax
 import jax.numpy as jnp
 from jax import lax
+from jax.experimental import pallas as pl
+from jax.experimental.pallas import tpu as pltpu
 from jax.sharding import PartitionSpec as P
 
-
-def body(amplitudes, integrals, occ_irrep, virt_irrep, occ_energy, virt_energy, slab_start):
+IRREPS = 8
+NX = 4
+CORES = 2
+SLOTS = 32
+HIGHEST = lax.Precision.HIGHEST
+MESH = pl.DeviceIdType.MESH
+NT = (((1,), (1,)), ((), ()))
+
+
+def iota(shape, axis):
+    return lax.broadcasted_iota(jnp.int32, shape, axis)
+
+
+def ring_order(ny):
+    order = [0]
+    for step in range(1, ny // 2):
+        order += [step, ny - step]
+    return order + [ny // 2]
+
+
+def kernel(
+    ny, nx, nz, slots, a_hbm, w_hbm, occ_s, virt_s, occ_en_s, virt_en_s, slab_s, occ_v, virt_v, occ_en_v,
+    out_ref, most_ref,
+    a_ref, w_ref, gath, part, core_out, core_in, acc, x_in, z_out, z_in, irrep_ref, slot_ref, energy_ref,
+    a_sem, w_sem, y_send, y_recv, core_send, core_recv, x_send, x_recv, z_send, z_recv,
+):
+    me_y = lax.axis_index("pair")
+    me_c = lax.axis_index("contr")
+    core = me_c % CORES
+    me_z = (me_c // CORES) % nz
+    me_x = me_c // (CORES * nz)
+    rows, depth = a_ref.shape
+    cols = w_ref.shape[1]
+    half = depth // 2
+    occ_count = occ_v.shape[1]
+    virt_count = virt_v.shape[1]
+    occ_pair = occ_count // ny
+    slab_first = rows // occ_pair
+    slab_second = cols // occ_pair
+    mine = rows // (nx * nz * CORES)
+    position = {d: p for p, d in enumerate(ring_order(ny))}
+    width = ny // 2 * slots
+
+    copy_w = pltpu.make_async_copy(w_hbm, w_ref, w_sem)
+    copy_w.start()
+    copy_a = pltpu.make_async_copy(a_hbm, a_ref, a_sem)
+    copy_a.start()
+
+    def at(x, z, k):
+        return (x * nz + z) * CORES + k
+
+    up = lax.rem(me_y + 1, ny)
+    down = lax.rem(me_y + ny - 1, ny)
+    other = at(me_x, me_z, 1 - core)
+
+    def x_peer(step):
+        return at(lax.rem(me_x + step, nx), me_z, core)
+
+    def z_peer(step):
+        return at(me_x, lax.rem(me_z + step, nz), core)
+
+    barrier = pltpu.get_barrier_semaphore()
+
+    def greet(y, c):
+        pl.semaphore_signal(barrier, inc=1, device_id=(y, c), device_id_type=MESH)
+
+    greet(up, me_c)
+    greet(down, me_c)
+    greet(me_y, other)
+    for step in range(1, nx):
+        greet(me_y, x_peer(step))
+
+    def greet_z(step, carry):
+        greet(me_y, z_peer(step))
+        return carry
+
+    lax.fori_loop(1, nz, greet_z, 0)
+
+    spread = jnp.where(iota((occ_count, cols), 0) % occ_pair == iota((occ_count, cols), 1) // slab_second, 1.0, 0.0)
+    own_row = iota((ny, occ_count), 1) // occ_pair == iota((ny, occ_count), 0)
+    b_at = iota((1, cols), 1) % slab_second
+    b_irrep = jnp.zeros((1, cols), jnp.int32)
+    b_energy = jnp.zeros((1, cols), jnp.float32)
+    for b in range(slab_second):
+        b_irrep = jnp.where(b_at == b, virt_s[slab_s[1] + b], b_irrep)
+        b_energy = jnp.where(b_at == b, virt_en_s[slab_s[1] + b], b_energy)
+    occ_row = occ_v[...]
+    col_occ = jnp.dot(jnp.where(own_row, occ_row.astype(jnp.float32), 0.0), spread, preferred_element_type=jnp.float32)
+    col_irrep = jnp.bitwise_xor(col_occ.astype(jnp.int32), b_irrep)
+    col_energy = jnp.dot(
+        jnp.where(own_row, occ_en_v[...], 0.0), spread, precision=HIGHEST, preferred_element_type=jnp.float32
+    ) - b_energy
+    before = jnp.where(iota((cols, cols), 0) < iota((cols, cols), 1), 1.0, 0.0)
+    hot = jnp.concatenate([jnp.where(col_irrep == g, 1.0, 0.0) for g in range(IRREPS)], axis=0)
+    counted = jnp.dot(hot, before, preferred_element_type=jnp.float32)
+    slot = jnp.zeros((ny, cols), jnp.float32)
+    for g in range(IRREPS):
+        slot = jnp.where(col_irrep == g, counted[g * ny : (g + 1) * ny], slot)
+    most_ref[0, 0] = jnp.max(slot)
+    slot = slot.astype(jnp.int32)
+    irrep_ref[...] = col_irrep
+    slot_ref[...] = slot
+    energy_ref[...] = col_energy
+
+    local_occ = depth // virt_count
+    kc_irrep = jnp.concatenate(
+        [jnp.bitwise_xor(virt_v[...], occ_s[me_c * local_occ + k]) for k in range(local_occ)], axis=1
+    )
+
+    key = irrep_ref[pl.ds(me_y, 1), :] * slots + slot_ref[pl.ds(me_y, 1), :]
+    pick = jnp.where(iota((IRREPS * slots, cols), 0) == key, 1.0, 0.0).astype(jnp.bfloat16)
+    copy_w.wait()
+    picked = lax.dot_general(pick, w_ref[...], NT, preferred_element_type=jnp.float32)
+    kept = picked[:slots]
+    for g in range(1, IRREPS):
+        kept = jnp.where(kc_irrep == g, picked[g * slots : (g + 1) * slots], kept)
+    kept = kept.astype(jnp.bfloat16)
+    for h in range(2):
+        gath[position[0], h] = kept[:, h * half : (h + 1) * half]
+
+    pl.semaphore_wait(barrier, 3 + (nx - 1) + (nz - 1))
+
+    def y_copy(src, dst, h, to):
+        return pltpu.make_async_remote_copy(
+            src_ref=gath.at[position[src], h],
+            dst_ref=gath.at[position[dst], h],
+            send_sem=y_send.at[2 * dst + h],
+            recv_sem=y_recv.at[2 * dst + h],
+            device_id=(to, me_c),
+            device_id_type=MESH,
+        )
+
+    y_copies = []
+
+    def forward(dst):
+        for turn in range(2):
+            for go_down in (True, False):
+                d = dst if go_down else ny - dst
+                h = turn if go_down else 1 - turn
+                src = d - 1 if go_down else (d + 1) % ny
+                if dst > 1:
+                    y_copy(src, src, h, down).wait_recv()
+                if dst == ny // 2 and turn == 1:
+                    continue
+                copy = y_copy(src, d, h, down if go_down else up)
+                copy.start()
+                y_copies.append(copy)
+
+    def arrived(dst):
+        for h in range(2):
+            for d in sorted({dst, ny - dst}):
+                y_copy(d, d, h, down).wait_recv()
+
+    def mask_amplitudes():
+        a_at = iota((slab_first, 128), 0)
+        a_irrep = jnp.zeros((slab_first, 128), jnp.int32)
+        for a in range(slab_first):
+            a_irrep = jnp.where(a_at == a, virt_s[slab_s[0] + a], a_irrep)
+        copy_a.wait()
+
+        def mask(i, carry):
+            at_rows = pl.ds(pl.multiple_of(i * slab_first, slab_first), slab_first)
+            row_irrep = jnp.bitwise_xor(a_irrep, occ_s[me_y * occ_pair + i])
+            row_irrep = jnp.concatenate([row_irrep] * (depth // 128), axis=1)
+            block = a_ref[at_rows, :].astype(jnp.float32)
+            a_ref[at_rows, :] = jnp.where(row_irrep == kc_irrep, block, 0.0).astype(jnp.bfloat16)
+            return carry
+
+        lax.fori_loop(0, occ_pair, mask, 0)
+
+    def multiply(group):
+        first = group * ny // 2
+        total = None
+        for h in range(2):
+            block = gath[first : first + ny // 2, h].reshape(width, half)
+            product = lax.dot_general(
+                a_ref[:, h * half : (h + 1) * half], block, NT, preferred_element_type=jnp.float32
+            )
+            total = product if total is None else total + product
+        part[group] = total
+        return send_core(group)
+
+    def strided(group, x, i, k):
+        first = (x * nz * CORES + k) * mine + i
+        return part[group, pl.ds(first, nz, stride=CORES * mine), :]
+
+    def send_core(group):
+        for x in range(nx):
+            for i in range(mine):
+                core_out[group, x, i * nz : (i + 1) * nz] = strided(group, x, i, 1 - core)
+        copy = pltpu.make_async_remote_copy(
+            src_ref=core_out.at[group],
+            dst_ref=core_in.at[group],
+            send_sem=core_send.at[group],
+            recv_sem=core_recv.at[group],
+            device_id=(me_y, other),
+            device_id_type=MESH,
+        )
+        copy.start()
+        for x in range(nx):
+            for i in range(mine):
+                acc[group, x, i * nz : (i + 1) * nz] = strided(group, x, i, core)
+        return copy
+
+    def send_x(group, copy):
+        copy.wait_recv()
+        acc[group] = acc[group] + core_in[group]
+        copies = []
+        for step in range(1, nx):
+            copies.append(
+                pltpu.make_async_remote_copy(
+                    src_ref=acc.at[group, lax.rem(me_x + step, nx)],
+                    dst_ref=x_in.at[group, step - 1],
+                    send_sem=x_send.at[group, step - 1],
+                    recv_sem=x_recv.at[group, step - 1],
+                    device_id=(me_y, x_peer(step)),
+                    device_id_type=MESH,
+                )
+            )
+            copies[-1].start()
+        return copies
+
+    def z_copy(group, step):
+        return pltpu.make_async_remote_copy(
+            src_ref=z_out.at[group, lax.rem(me_z + step, nz)],
+            dst_ref=z_in.at[group, step - 1],
+            send_sem=z_send.at[group, step - 1],
+            recv_sem=z_recv.at[group, step - 1],
+            device_id=(me_y, z_peer(step)),
+            device_id_type=MESH,
+        )
+
+    def send_z(group, copies):
+        total = acc[group, me_x]
+        for copy in copies:
+            copy.wait_recv()
+        for step in range(nx - 1):
+            total = total + x_in[group, step]
+        for i in range(mine):
+            z_out[group, :, i, :] = total[i * nz : (i + 1) * nz]
+
+        def go(step, carry):
+            z_copy(group, step).start()
+            return carry
+
+        lax.fori_loop(1, nz, go, 0)
+
+    def finish(group):
+        def ready(step, carry):
+            z_copy(group, step).wait_recv()
+            return carry
+
+        lax.fori_loop(1, nz, ready, 0)
+        total = z_out[group, me_z]
+        for step in range(nz - 1):
+            total = total + z_in[group, step]
+        blocks = [lax.rem(me_y + d, ny) for d in ring_order(ny)[group * ny // 2 : (group + 1) * ny // 2]]
+        seat = iota((width, cols), 0)
+        place = jnp.concatenate(
+            [
+                jnp.where(slot_ref[pl.ds(block, 1), :] + p * slots == seat, 1.0, 0.0)
+                for p, block in enumerate(blocks)
+            ],
+            axis=1,
+        )
+        placed = jnp.dot(total, place, precision=HIGHEST, preferred_element_type=jnp.float32)
+        for p, block in enumerate(blocks):
+            value = placed[:, p * cols : (p + 1) * cols]
+            cycle = jnp.where(row_irrep == irrep_ref[pl.ds(block, 1), :], value, 0.0)
+            update = cycle / (row_energy + energy_ref[pl.ds(block, 1), :])
+            out_ref[:, pl.ds(pl.multiple_of(block * cols, cols), cols)] = update.astype(out_ref.dtype)
+
+    row_first = me_c * mine
+    row_occ = me_y * occ_pair + row_first // slab_first
+    row_virt = row_first % slab_first
+    row_at = iota((mine, cols), 0)
+    row_irrep = jnp.zeros((mine, cols), jnp.int32)
+    row_energy = jnp.zeros((mine, cols), jnp.float32)
+    for i in range(mine):
+        a = slab_s[0] + row_virt + i
+        row_irrep = jnp.where(row_at == i, jnp.bitwise_xor(occ_s[row_occ], virt_s[a]), row_irrep)
+        row_energy = jnp.where(row_at == i, occ_en_s[row_occ] - virt_en_s[a], row_energy)
+
+    forward(1)
+    mask_amplitudes()
+    for dst in range(2, ny // 2):
+        forward(dst)
+    core_first = multiply(0)
+    forward(ny // 2)
+    x_first = send_x(0, core_first)
+    arrived(ny // 2)
+    core_second = multiply(1)
+    send_z(0, x_first)
+    x_second = send_x(1, core_second)
+    finish(0)
+    send_z(1, x_second)
+    finish(1)
+
+    for copy in y_copies + [core_first, core_second] + x_first + x_second:
+        copy.wait_send()
+
+    def sent(step, carry):
+        for group in range(2):
+            z_copy(group, step).wait_send()
+        return carry
+
+    lax.fori_loop(1, nz, sent, 0)
+
+
+def contract(amplitudes, integrals, occ_irrep, virt_irrep, occ_energy, virt_energy, slab_start, slots):
+    ny = lax.axis_size("pair")
+    nx = NX
+    nz = lax.axis_size("contr") // (nx * CORES)
+    rows, depth = amplitudes.shape
+    cols = integrals.shape[1]
+    mine = rows // (nx * nz * CORES)
+    width = ny // 2 * slots
+    smem = pl.BlockSpec(memory_space=pltpu.SMEM)
+    vmem = pl.BlockSpec(memory_space=pltpu.VMEM)
+    anywhere = pl.BlockSpec(memory_space=pl.ANY)
+    f32 = jnp.float32
+    bf16 = jnp.bfloat16
+    dma = pltpu.SemaphoreType.DMA
+    return pl.pallas_call(
+        functools.partial(kernel, ny, nx, nz, slots),
+        out_shape=(
+            jax.ShapeDtypeStruct((mine, cols * ny), bf16),
+            jax.ShapeDtypeStruct((1, 1), f32),
+        ),
+        in_specs=[anywhere, anywhere] + [smem] * 5 + [vmem] * 3,
+        out_specs=(vmem, smem),
+        scratch_shapes=[
+            pltpu.VMEM((rows, depth), bf16),
+            pltpu.VMEM((depth, cols), bf16),
+            pltpu.VMEM((ny, 2, slots, depth // 2), bf16),
+            pltpu.VMEM((2, rows, width), f32),
+            pltpu.VMEM((2, nx, mine * nz, width), f32),
+            pltpu.VMEM((2, nx, mine * nz, width), f32),
+            pltpu.VMEM((2, nx, mine * nz, width), f32),
+            pltpu.VMEM((2, nx - 1, mine * nz, width), f32),
+            pltpu.VMEM((2, nz, mine, width), f32),
+            pltpu.VMEM((2, nz - 1, mine, width), f32),
+            pltpu.VMEM((ny, cols), jnp.int32),
+            pltpu.VMEM((ny, cols), jnp.int32),
+            pltpu.VMEM((ny, cols), f32),
+            dma,
+            dma,
+            dma((2 * ny,)),
+            dma((2 * ny,)),
+            dma((2,)),
+            dma((2,)),
+            dma((2, nx - 1)),
+            dma((2, nx - 1)),
+            dma((2, nz - 1)),
+            dma((2, nz - 1)),
+        ],
+        compiler_params=pltpu.CompilerParams(
+            collective_id=0, has_side_effects=True, vmem_limit_bytes=32 * 1024 * 1024
+        ),
+        cost_estimate=pl.CostEstimate(
+            flops=2 * rows * depth * width * 2, bytes_accessed=2 * depth * (rows + cols), transcendentals=0
+        ),
+    )(
+        amplitudes,
+        integrals,
+        occ_irrep,
+        virt_irrep,
+        occ_energy,
+        virt_energy,
+        slab_start,
+        occ_irrep[None, :],
+        virt_irrep[None, :],
+        occ_energy[None, :],
+    )
+
+
+def dense(amplitudes, integrals, occ_irrep, virt_irrep, occ_energy, virt_energy, slab_start):
     pair_count = lax.axis_size("pair")
     contr_count = lax.axis_size("contr")
     pair_index = lax.axis_index("pair")
@@ -17,12 +396,10 @@
     rows_device = rows_pair // contr_count
     slab_first = amplitudes.shape[0] * pair_count // occ_irrep.shape[0]
     slab_second = cols_pair * pair_count // occ_irrep.shape[0]
-    first_start = slab_start[0]
-    second_start = slab_start[1]
-    a_irrep = lax.dynamic_slice(virt_irrep, (first_start,), (slab_first,))
-    b_irrep = lax.dynamic_slice(virt_irrep, (second_start,), (slab_second,))
-    a_energy = lax.dynamic_slice(virt_energy, (first_start,), (slab_first,))
-    b_energy = lax.dynamic_slice(virt_energy, (second_start,), (slab_second,))
+    a_irrep = lax.dynamic_slice(virt_irrep, (slab_start[0],), (slab_first,))
+    b_irrep = lax.dynamic_slice(virt_irrep, (slab_start[1],), (slab_second,))
+    a_energy = lax.dynamic_slice(virt_energy, (slab_start[0],), (slab_first,))
+    b_energy = lax.dynamic_slice(virt_energy, (slab_start[1],), (slab_second,))
     row_irrep = jnp.bitwise_xor(occ_irrep[:, None], a_irrep[None, :]).reshape(-1)
     col_irrep = jnp.bitwise_xor(occ_irrep[:, None], b_irrep[None, :]).reshape(-1)
     row_energy = (occ_energy[:, None] - a_energy[None, :]).reshape(-1)
@@ -43,8 +420,12 @@
     mine_energy = lax.dynamic_slice(
         row_energy, (pair_index * rows_pair + contr_index * rows_device,), (rows_device,)
     )
-    update = (summed / (mine_energy[:, None] + col_energy[None, :])).astype(jnp.bfloat16)
-    return update
+    return (summed / (mine_energy[:, None] + col_energy[None, :])).astype(jnp.bfloat16)
+
+
+def body(*args):
+    update, most = contract(*args, slots=SLOTS)
+    return lax.cond(most[0, 0] > SLOTS - 1, lambda: dense(*args), lambda: update)
 
 
 def solution(mesh):

time: 448 us -> 69.4 us (0.15)
  the two profiles are of different devices: /device:TPU:1 before, /device:TPU:8 now
where the time goes in v1:
time: 69.4 us; the launch traced here: 69.2 us
  Pallas kernels  54.6 us (79%)
  between operations  14 us (20%)
    pallas_call x1, Pallas kernels, contract(): pl.pallas_call(functools.partial(kernel, ny, nx, nz, slots), out_shape=(j...  54.6 us

profile of v1, /device:TPU:8, one launch (start us, length us, event | category | flops | bytes accessed | tf_op | source)
XLA Modules:
  0.0 69.2 jit_solution(9132259976538713811)
XLA Ops:
  6.5 54.6 %shard_map.75 = (bf16[4,1024]{1,0:T(4,128)(2,1)S(1)}, f32[1,1]{1,0:T(1,128)}) custom-call(bf16[512,1024]{1,0:T(8,128)(2,1)} %a_hbm.1, bf16[1024,128]{1,0:T(8,128)(2,1)} %w_hbm.1, s32[256]{0:T(256)} %occ_s.1, s32[512]{0:T(512)} %virt_s.1, f32[256]{0:T(256)} %occ_en_s.1, f32[512]{0:T(512)} %virt_en_s.1, s32[2]{0:T(128)} %slab_s.1, s32[1,256]{1,0:T(1,128)} %bitcast.11, ...), custom_call_target="tpu_custom_call" | custom-call | flops 268435456 | bytes 1310720 | tf_op jit(solution)/shard_map/pallas_call | solution.py:333
  61.8 0.6 copy.15
  (1 shorter events, 0.0 us)

commit v2 on v1

--- a/solution.py
+++ b/solution.py
@@ -28,10 +28,11 @@
 
 
 def kernel(
-    ny, nx, nz, slots, a_hbm, w_hbm, occ_s, virt_s, occ_en_s, virt_en_s, slab_s, occ_v, virt_v, occ_en_v,
+    ny, nx, nz, slots, a_hbm, w_hbm, occ_hbm, virt_hbm, occ_en_hbm, virt_en_hbm, slab_hbm,
     out_ref, most_ref,
-    a_ref, w_ref, gath, part, core_out, core_in, acc, x_in, z_out, z_in, irrep_ref, slot_ref, energy_ref,
-    a_sem, w_sem, y_send, y_recv, core_send, core_recv, x_send, x_recv, z_send, z_recv,
+    a_ref, w_ref, occ_s, virt_s, occ_en_s, virt_en_s, slab_s, occ_v, virt_v, occ_en_v,
+    gath, part, core_out, core_in, acc, x_in, z_out, z_in, irrep_ref, slot_ref, energy_ref, place_ref,
+    in_sem, y_send, y_recv, core_send, core_recv, x_send, x_recv, z_send, z_recv, known_sem,
 ):
     me_y = lax.axis_index("pair")
     me_c = lax.axis_index("contr")
@@ -50,16 +51,9 @@
     position = {d: p for p, d in enumerate(ring_order(ny))}
     width = ny // 2 * slots
 
-    copy_w = pltpu.make_async_copy(w_hbm, w_ref, w_sem)
-    copy_w.start()
-    copy_a = pltpu.make_async_copy(a_hbm, a_ref, a_sem)
-    copy_a.start()
-
     def at(x, z, k):
         return (x * nz + z) * CORES + k
 
-    up = lax.rem(me_y + 1, ny)
-    down = lax.rem(me_y + ny - 1, ny)
     other = at(me_x, me_z, 1 - core)
 
     def x_peer(step):
@@ -68,37 +62,66 @@
     def z_peer(step):
         return at(me_x, lax.rem(me_z + step, nz), core)
 
+    def near(count, *steps):
+        return sorted({step % count for most in steps for step in (most, -most)} - {0})
+
     barrier = pltpu.get_barrier_semaphore()
-
-    def greet(y, c):
-        pl.semaphore_signal(barrier, inc=1, device_id=(y, c), device_id_type=MESH)
-
-    greet(up, me_c)
-    greet(down, me_c)
-    greet(me_y, other)
-    for step in range(1, nx):
-        greet(me_y, x_peer(step))
-
-    def greet_z(step, carry):
-        greet(me_y, z_peer(step))
-        return carry
-
-    lax.fori_loop(1, nz, greet_z, 0)
+    greeted = [(lax.rem(me_y + step, ny), me_c) for step in near(ny, 1, 2)]
+    greeted += [(me_y, other)]
+    greeted += [(me_y, x_peer(step)) for step in near(nx, 1, 2)]
+    greeted += [(me_y, z_peer(step)) for step in near(nz, 1, 2)]
+    for device in greeted:
+        pl.semaphore_signal(barrier, inc=1, device_id=device, device_id_type=MESH)
+
+    copies_in = [
+        pltpu.make_async_copy(src, dst, in_sem.at[i])
+        for i, (src, dst) in enumerate(
+            [
+                (occ_hbm, occ_s),
+                (virt_hbm, virt_s),
+                (slab_hbm, slab_s),
+                (occ_hbm, occ_v),
+                (virt_hbm, virt_v),
+                (w_hbm, w_ref),
+                (a_hbm, a_ref),
+                (occ_en_hbm, occ_en_s),
+                (virt_en_hbm, virt_en_s),
+                (occ_en_hbm, occ_en_v),
+            ]
+        )
+    ]
+    for copy in copies_in:
+        copy.start()
+    copy_w, copy_a = copies_in[5:7]
+
+    relays = []
+    reach = 2
+    while 2 * reach <= nz // 2:
+        relays.append(reach)
+        reach *= 2
+
+    def relay(level):
+        if level < len(relays):
+            for step in near(nz, relays[level]):
+                pl.semaphore_signal(
+                    known_sem.at[level], inc=1, device_id=(me_y, z_peer(step)), device_id_type=MESH
+                )
+
+    def relayed(level):
+        if level < len(relays):
+            pl.semaphore_wait(known_sem.at[level], len(near(nz, relays[level])))
 
     spread = jnp.where(iota((occ_count, cols), 0) % occ_pair == iota((occ_count, cols), 1) // slab_second, 1.0, 0.0)
     own_row = iota((ny, occ_count), 1) // occ_pair == iota((ny, occ_count), 0)
     b_at = iota((1, cols), 1) % slab_second
+    for copy in copies_in[:5]:
+        copy.wait()
     b_irrep = jnp.zeros((1, cols), jnp.int32)
-    b_energy = jnp.zeros((1, cols), jnp.float32)
     for b in range(slab_second):
-        b_irrep = jnp.where(b_at == b, virt_s[slab_s[1] + b], b_irrep)
-        b_energy = jnp.where(b_at == b, virt_en_s[slab_s[1] + b], b_energy)
+        b_irrep = jnp.where(b_at == b, virt_s[0, slab_s[0, 1] + b], b_irrep)
     occ_row = occ_v[...]
     col_occ = jnp.dot(jnp.where(own_row, occ_row.astype(jnp.float32), 0.0), spread, preferred_element_type=jnp.float32)
     col_irrep = jnp.bitwise_xor(col_occ.astype(jnp.int32), b_irrep)
-    col_energy = jnp.dot(
-        jnp.where(own_row, occ_en_v[...], 0.0), spread, precision=HIGHEST, preferred_element_type=jnp.float32
-    ) - b_energy
     before = jnp.where(iota((cols, cols), 0) < iota((cols, cols), 1), 1.0, 0.0)
     hot = jnp.concatenate([jnp.where(col_irrep == g, 1.0, 0.0) for g in range(IRREPS)], axis=0)
     counted = jnp.dot(hot, before, preferred_element_type=jnp.float32)
@@ -109,11 +132,10 @@
     slot = slot.astype(jnp.int32)
     irrep_ref[...] = col_irrep
     slot_ref[...] = slot
-    energy_ref[...] = col_energy
 
     local_occ = depth // virt_count
     kc_irrep = jnp.concatenate(
-        [jnp.bitwise_xor(virt_v[...], occ_s[me_c * local_occ + k]) for k in range(local_occ)], axis=1
+        [jnp.bitwise_xor(virt_v[...], occ_s[0, me_c * local_occ + k]) for k in range(local_occ)], axis=1
     )
 
     key = irrep_ref[pl.ds(me_y, 1), :] * slots + slot_ref[pl.ds(me_y, 1), :]
@@ -127,49 +149,47 @@
     for h in range(2):
         gath[position[0], h] = kept[:, h * half : (h + 1) * half]
 
-    pl.semaphore_wait(barrier, 3 + (nx - 1) + (nz - 1))
-
-    def y_copy(src, dst, h, to):
+    pl.semaphore_wait(barrier, len(greeted))
+
+    def y_copy(src, dst, h, step):
         return pltpu.make_async_remote_copy(
             src_ref=gath.at[position[src], h],
             dst_ref=gath.at[position[dst], h],
             send_sem=y_send.at[2 * dst + h],
             recv_sem=y_recv.at[2 * dst + h],
-            device_id=(to, me_c),
+            device_id=(lax.rem(me_y + step % ny, ny), me_c),
             device_id_type=MESH,
         )
 
     y_copies = []
 
-    def forward(dst):
-        for turn in range(2):
-            for go_down in (True, False):
-                d = dst if go_down else ny - dst
-                h = turn if go_down else 1 - turn
-                src = d - 1 if go_down else (d + 1) % ny
-                if dst > 1:
-                    y_copy(src, src, h, down).wait_recv()
-                if dst == ny // 2 and turn == 1:
-                    continue
-                copy = y_copy(src, d, h, down if go_down else up)
-                copy.start()
-                y_copies.append(copy)
-
-    def arrived(dst):
-        for h in range(2):
-            for d in sorted({dst, ny - dst}):
-                y_copy(d, d, h, down).wait_recv()
+    def send_y(src, dst, turn):
+        for sign in (1, -1):
+            h = turn if sign == 1 else 1 - turn
+            y_copies.append(y_copy(sign * src % ny, sign * dst % ny, h, sign * (src - dst)))
+            y_copies[-1].start()
+
+    def arrived(dst, turns=(0, 1)):
+        for turn in turns:
+            for sign in (1, -1):
+                h = turn if sign == 1 else 1 - turn
+                y_copy(sign * dst % ny, sign * dst % ny, h, 1).wait_recv()
+
+    for turn in range(2):
+        send_y(0, 2, turn)
+        send_y(0, 1, turn)
+    relay(0)
 
     def mask_amplitudes():
         a_at = iota((slab_first, 128), 0)
         a_irrep = jnp.zeros((slab_first, 128), jnp.int32)
         for a in range(slab_first):
-            a_irrep = jnp.where(a_at == a, virt_s[slab_s[0] + a], a_irrep)
+            a_irrep = jnp.where(a_at == a, virt_s[0, slab_s[0, 0] + a], a_irrep)
         copy_a.wait()
 
         def mask(i, carry):
             at_rows = pl.ds(pl.multiple_of(i * slab_first, slab_first), slab_first)
-            row_irrep = jnp.bitwise_xor(a_irrep, occ_s[me_y * occ_pair + i])
+            row_irrep = jnp.bitwise_xor(a_irrep, occ_s[0, me_y * occ_pair + i])
             row_irrep = jnp.concatenate([row_irrep] * (depth // 128), axis=1)
             block = a_ref[at_rows, :].astype(jnp.float32)
             a_ref[at_rows, :] = jnp.where(row_irrep == kc_irrep, block, 0.0).astype(jnp.bfloat16)
@@ -215,7 +235,7 @@
         copy.wait_recv()
         acc[group] = acc[group] + core_in[group]
         copies = []
-        for step in range(1, nx):
+        for step in sorted(range(1, nx), key=lambda step: -min(step, nx - step)):
             copies.append(
                 pltpu.make_async_remote_copy(
                     src_ref=acc.at[group, lax.rem(me_x + step, nx)],
@@ -248,37 +268,49 @@
         for i in range(mine):
             z_out[group, :, i, :] = total[i * nz : (i + 1) * nz]
 
-        def go(step, carry):
-            z_copy(group, step).start()
-            return carry
-
-        lax.fori_loop(1, nz, go, 0)
-
-    def finish(group):
-        def ready(step, carry):
-            z_copy(group, step).wait_recv()
-            return carry
-
-        lax.fori_loop(1, nz, ready, 0)
+        copies = [z_copy(group, step) for step in sorted(range(1, nz), key=lambda step: -min(step, nz - step))]
+        for copy in copies:
+            copy.start()
+        return copies
+
+    def finish(group, copies):
+        for copy in copies:
+            copy.wait_recv()
         total = z_out[group, me_z]
         for step in range(nz - 1):
             total = total + z_in[group, step]
-        blocks = [lax.rem(me_y + d, ny) for d in ring_order(ny)[group * ny // 2 : (group + 1) * ny // 2]]
-        seat = iota((width, cols), 0)
-        place = jnp.concatenate(
-            [
-                jnp.where(slot_ref[pl.ds(block, 1), :] + p * slots == seat, 1.0, 0.0)
-                for p, block in enumerate(blocks)
-            ],
-            axis=1,
+        high = total.astype(jnp.bfloat16)
+        rest = total - high.astype(jnp.float32)
+        middle = rest.astype(jnp.bfloat16)
+        low = (rest - middle.astype(jnp.float32)).astype(jnp.bfloat16)
+        placed = sum(
+            jnp.dot(term, place_ref[group], preferred_element_type=jnp.float32) for term in (low, middle, high)
         )
-        placed = jnp.dot(total, place, precision=HIGHEST, preferred_element_type=jnp.float32)
+        blocks = group_blocks(group)
         for p, block in enumerate(blocks):
             value = placed[:, p * cols : (p + 1) * cols]
             cycle = jnp.where(row_irrep == irrep_ref[pl.ds(block, 1), :], value, 0.0)
             update = cycle / (row_energy + energy_ref[pl.ds(block, 1), :])
             out_ref[:, pl.ds(pl.multiple_of(block * cols, cols), cols)] = update.astype(out_ref.dtype)
 
+    def group_blocks(group):
+        return [lax.rem(me_y + d, ny) for d in ring_order(ny)[group * ny // 2 : (group + 1) * ny // 2]]
+
+    mask_amplitudes()
+
+    seat = iota((width, cols), 0)
+    for group in range(2):
+        for p, block in enumerate(group_blocks(group)):
+            placing = jnp.where(slot_ref[pl.ds(block, 1), :] + p * slots == seat, 1.0, 0.0)
+            place_ref[group, :, p * cols : (p + 1) * cols] = placing.astype(jnp.bfloat16)
+    for copy in copies_in[7:]:
+        copy.wait()
+    b_energy = jnp.zeros((1, cols), jnp.float32)
+    for b in range(slab_second):
+        b_energy = jnp.where(b_at == b, virt_en_s[0, slab_s[0, 1] + b], b_energy)
+    energy_ref[...] = jnp.dot(
+        jnp.where(own_row, occ_en_v[...], 0.0), spread, precision=HIGHEST, preferred_element_type=jnp.float32
+    ) - b_energy
     row_first = me_c * mine
     row_occ = me_y * occ_pair + row_first // slab_first
     row_virt = row_first % slab_first
@@ -286,37 +318,36 @@
     row_irrep = jnp.zeros((mine, cols), jnp.int32)
     row_energy = jnp.zeros((mine, cols), jnp.float32)
     for i in range(mine):
-        a = slab_s[0] + row_virt + i
-        row_irrep = jnp.where(row_at == i, jnp.bitwise_xor(occ_s[row_occ], virt_s[a]), row_irrep)
-        row_energy = jnp.where(row_at == i, occ_en_s[row_occ] - virt_en_s[a], row_energy)
-
-    forward(1)
-    mask_amplitudes()
-    for dst in range(2, ny // 2):
-        forward(dst)
+        a = slab_s[0, 0] + row_virt + i
+        row_irrep = jnp.where(row_at == i, jnp.bitwise_xor(occ_s[0, row_occ], virt_s[0, a]), row_irrep)
+        row_energy = jnp.where(row_at == i, occ_en_s[0, row_occ] - virt_en_s[0, a], row_energy)
+
+    arrived(1, (0,))
+    send_y(1, 3, 0)
+    arrived(2, (0,))
+    send_y(2, 4, 0)
+    arrived(1, (1,))
+    send_y(1, 3, 1)
+    relayed(0)
+    relay(1)
+    arrived(2, (1,))
     core_first = multiply(0)
-    forward(ny // 2)
+    relayed(1)
     x_first = send_x(0, core_first)
-    arrived(ny // 2)
+    arrived(3)
+    arrived(4, (0,))
     core_second = multiply(1)
-    send_z(0, x_first)
+    z_first = send_z(0, x_first)
     x_second = send_x(1, core_second)
-    finish(0)
-    send_z(1, x_second)
-    finish(1)
-
-    for copy in y_copies + [core_first, core_second] + x_first + x_second:
+    z_second = send_z(1, x_second)
+    finish(0, z_first)
+    finish(1, z_second)
+
+    for copy in y_copies + [core_first, core_second] + x_first + x_second + z_first + z_second:
         copy.wait_send()
 
-    def sent(step, carry):
-        for group in range(2):
-            z_copy(group, step).wait_send()
-        return carry
-
-    lax.fori_loop(1, nz, sent, 0)
-
-
-def contract(amplitudes, integrals, occ_irrep, virt_irrep, occ_energy, virt_energy, slab_start, slots):
+
+def contract(amplitudes, integrals, occ_irrep, virt_irrep, occ_energy, virt_energy, slab_start, slots, collective_id=0):
     ny = lax.axis_size("pair")
     nx = NX
     nz = lax.axis_size("contr") // (nx * CORES)
@@ -336,11 +367,19 @@
             jax.ShapeDtypeStruct((mine, cols * ny), bf16),
             jax.ShapeDtypeStruct((1, 1), f32),
         ),
-        in_specs=[anywhere, anywhere] + [smem] * 5 + [vmem] * 3,
+        in_specs=[anywhere] * 7,
         out_specs=(vmem, smem),
         scratch_shapes=[
             pltpu.VMEM((rows, depth), bf16),
             pltpu.VMEM((depth, cols), bf16),
+            pltpu.SMEM((1, occ_irrep.shape[0]), jnp.int32),
+            pltpu.SMEM((1, virt_irrep.shape[0]), jnp.int32),
+            pltpu.SMEM((1, occ_irrep.shape[0]), f32),
+            pltpu.SMEM((1, virt_irrep.shape[0]), f32),
+            pltpu.SMEM((1, slab_start.shape[0]), jnp.int32),
+            pltpu.VMEM((1, occ_irrep.shape[0]), jnp.int32),
+            pltpu.VMEM((1, virt_irrep.shape[0]), jnp.int32),
+            pltpu.VMEM((1, occ_irrep.shape[0]), f32),
             pltpu.VMEM((ny, 2, slots, depth // 2), bf16),
             pltpu.VMEM((2, rows, width), f32),
             pltpu.VMEM((2, nx, mine * nz, width), f32),
@@ -352,8 +391,8 @@
             pltpu.VMEM((ny, cols), jnp.int32),
             pltpu.VMEM((ny, cols), jnp.int32),
             pltpu.VMEM((ny, cols), f32),
-            dma,
-            dma,
+            pltpu.VMEM((2, width, ny // 2 * cols), bf16),
+            dma((10,)),
             dma((2 * ny,)),
             dma((2 * ny,)),
             dma((2,)),
@@ -362,9 +401,10 @@
             dma((2, nx - 1)),
             dma((2, nz - 1)),
             dma((2, nz - 1)),
+            pltpu.SemaphoreType.REGULAR((2,)),
         ],
         compiler_params=pltpu.CompilerParams(
-            collective_id=0, has_side_effects=True, vmem_limit_bytes=32 * 1024 * 1024
+            collective_id=collective_id, has_side_effects=True, vmem_limit_bytes=32 * 1024 * 1024
         ),
         cost_estimate=pl.CostEstimate(
             flops=2 * rows * depth * width * 2, bytes_accessed=2 * depth * (rows + cols), transcendentals=0
@@ -372,14 +412,11 @@
     )(
         amplitudes,
         integrals,
-        occ_irrep,
-        virt_irrep,
-        occ_energy,
-        virt_energy,
-        slab_start,
         occ_irrep[None, :],
         virt_irrep[None, :],
         occ_energy[None, :],
+        virt_energy[None, :],
+        slab_start[None, :],
     )
 
 

time: 69.4 us -> 60.8 us (0.88)
  Pallas kernels: 54.6 us -> 46 us
    pallas_call x1, Pallas kernels: 54.6 us -> 46 us  [contract(): pl.pallas_call(functools.partial(kernel, ny, nx, nz, slots), out_shape=(j...]
where the time goes in v2:
time: 60.8 us; the launch traced here: 60.6 us
  Pallas kernels  46 us (76%)
  between operations  14 us (23%)
    pallas_call x1, Pallas kernels, contract(): pl.pallas_call(functools.partial(kernel, ny, nx, nz, slots), out_shape=(j...  46 us

profile of v2, /device:TPU:8, one launch (start us, length us, event | category | flops | bytes accessed | tf_op | source)
XLA Modules:
  0.0 60.6 jit_solution(6029300820765571501)
XLA Ops:
  6.5 46.0 %shard_map.75 = (bf16[4,1024]{1,0:T(4,128)(2,1)S(1)}, f32[1,1]{1,0:T(1,128)}) custom-call(bf16[512,1024]{1,0:T(8,128)(2,1)} %a_hbm.1, bf16[1024,128]{1,0:T(8,128)(2,1)} %w_hbm.1, s32[1,256]{1,0:T(1,128)} %bitcast.12, s32[1,512]{1,0:T(1,128)} %bitcast.14, f32[1,256]{1,0:T(1,128)} %bitcast.13, f32[1,512]{1,0:T(1,128)} %bitcast.17, s32[1,2]{1,0:T(1,128)} %bitcast.15), custom_call_target="tpu_custom_call" | custom-call | flops 268435456 | bytes 1310720 | tf_op jit(solution)/shard_map/pallas_call | solution.py:364
  53.2 0.6 copy.15
  (1 shorter events, 0.0 us)

commit v3 on v2

--- a/solution.py
+++ b/solution.py
@@ -206,12 +206,14 @@
                 a_ref[:, h * half : (h + 1) * half], block, NT, preferred_element_type=jnp.float32
             )
             total = product if total is None else total + product
-        part[group] = total
+        for t in range(width // 128):
+            part[group, t] = total[:, t * 128 : (t + 1) * 128]
         return send_core(group)
 
     def strided(group, x, i, k):
         first = (x * nz * CORES + k) * mine + i
-        return part[group, pl.ds(first, nz, stride=CORES * mine), :]
+        at_rows = pl.ds(first, nz, stride=CORES * mine)
+        return jnp.concatenate([part[group, t, at_rows, :] for t in range(width // 128)], axis=1)
 
     def send_core(group):
         for x in range(nx):
@@ -357,7 +359,7 @@
     width = ny // 2 * slots
     smem = pl.BlockSpec(memory_space=pltpu.SMEM)
     vmem = pl.BlockSpec(memory_space=pltpu.VMEM)
-    anywhere = pl.BlockSpec(memory_space=pl.ANY)
+    hbm = pl.BlockSpec(memory_space=pltpu.HBM)
     f32 = jnp.float32
     bf16 = jnp.bfloat16
     dma = pltpu.SemaphoreType.DMA
@@ -367,7 +369,7 @@
             jax.ShapeDtypeStruct((mine, cols * ny), bf16),
             jax.ShapeDtypeStruct((1, 1), f32),
         ),
-        in_specs=[anywhere] * 7,
+        in_specs=[hbm] * 7,
         out_specs=(vmem, smem),
         scratch_shapes=[
             pltpu.VMEM((rows, depth), bf16),
@@ -381,7 +383,7 @@
             pltpu.VMEM((1, virt_irrep.shape[0]), jnp.int32),
             pltpu.VMEM((1, occ_irrep.shape[0]), f32),
             pltpu.VMEM((ny, 2, slots, depth // 2), bf16),
-            pltpu.VMEM((2, rows, width), f32),
+            pltpu.VMEM((2, width // 128, rows, 128), f32),
             pltpu.VMEM((2, nx, mine * nz, width), f32),
             pltpu.VMEM((2, nx, mine * nz, width), f32),
             pltpu.VMEM((2, nx, mine * nz, width), f32),
@@ -404,7 +406,7 @@
             pltpu.SemaphoreType.REGULAR((2,)),
         ],
         compiler_params=pltpu.CompilerParams(
-            collective_id=collective_id, has_side_effects=True, vmem_limit_bytes=32 * 1024 * 1024
+            collective_id=collective_id, has_side_effects=True, vmem_limit_bytes=60 * 1024 * 1024
         ),
         cost_estimate=pl.CostEstimate(
             flops=2 * rows * depth * width * 2, bytes_accessed=2 * depth * (rows + cols), transcendentals=0
@@ -420,49 +422,13 @@
     )
 
 
-def dense(amplitudes, integrals, occ_irrep, virt_irrep, occ_energy, virt_energy, slab_start):
-    pair_count = lax.axis_size("pair")
-    contr_count = lax.axis_size("contr")
-    pair_index = lax.axis_index("pair")
-    contr_index = lax.axis_index("contr")
-    virt_count = virt_irrep.shape[0]
-    kc_local = integrals.shape[0]
-    occ_local = kc_local // virt_count
-    rows_pair = amplitudes.shape[0]
-    cols_pair = integrals.shape[1]
-    rows_device = rows_pair // contr_count
-    slab_first = amplitudes.shape[0] * pair_count // occ_irrep.shape[0]
-    slab_second = cols_pair * pair_count // occ_irrep.shape[0]
-    a_irrep = lax.dynamic_slice(virt_irrep, (slab_start[0],), (slab_first,))
-    b_irrep = lax.dynamic_slice(virt_irrep, (slab_start[1],), (slab_second,))
-    a_energy = lax.dynamic_slice(virt_energy, (slab_start[0],), (slab_first,))
-    b_energy = lax.dynamic_slice(virt_energy, (slab_start[1],), (slab_second,))
-    row_irrep = jnp.bitwise_xor(occ_irrep[:, None], a_irrep[None, :]).reshape(-1)
-    col_irrep = jnp.bitwise_xor(occ_irrep[:, None], b_irrep[None, :]).reshape(-1)
-    row_energy = (occ_energy[:, None] - a_energy[None, :]).reshape(-1)
-    col_energy = (occ_energy[:, None] - b_energy[None, :]).reshape(-1)
-    local_occ = lax.dynamic_slice(occ_irrep, (contr_index * occ_local,), (occ_local,))
-    kc_irrep = jnp.bitwise_xor(local_occ[:, None], virt_irrep[None, :]).reshape(-1)
-    zero = jnp.zeros((), jnp.bfloat16)
-    whole_int = lax.all_gather(integrals, "pair", axis=1, tiled=True)
-    int_masked = jnp.where(kc_irrep[:, None] == col_irrep[None, :], whole_int, zero)
-    row_irrep_pair = lax.dynamic_slice(row_irrep, (pair_index * rows_pair,), (rows_pair,))
-    amp_masked = jnp.where(row_irrep_pair[:, None] == kc_irrep[None, :], amplitudes, zero)
-    summed = lax.psum_scatter(
-        jnp.dot(amp_masked, int_masked, preferred_element_type=jnp.float32),
-        "contr",
-        scatter_dimension=0,
-        tiled=True,
+def body(*args):
+    update, most = contract(*args, slots=SLOTS, collective_id=0)
+    return lax.cond(
+        most[0, 0] > SLOTS - 1,
+        lambda: contract(*args, slots=args[1].shape[1], collective_id=1)[0],
+        lambda: update,
     )
-    mine_energy = lax.dynamic_slice(
-        row_energy, (pair_index * rows_pair + contr_index * rows_device,), (rows_device,)
-    )
-    return (summed / (mine_energy[:, None] + col_energy[None, :])).astype(jnp.bfloat16)
-
-
-def body(*args):
-    update, most = contract(*args, slots=SLOTS)
-    return lax.cond(most[0, 0] > SLOTS - 1, lambda: dense(*args), lambda: update)
 
 
 def solution(mesh):

time: 60.8 us -> 48.2 us (0.79)
  between operations: 14 us -> 0.71 us
  local copies, waits for them, and re-layouts: 0.6 us -> 1.25 us
    unnamed x1 -> x15, local copies, waits for them, and re-layouts: 0.6 us -> 1.25 us
where the time goes in v3:
time: 48.2 us; the launch traced here: 48.1 us
  Pallas kernels  46.1 us (96%)
  local copies, waits for them, and re-layouts  1.25 us (3%)
  between operations  0.71 us (1%)
    pallas_call x1, Pallas kernels, contract(): pl.pallas_call(functools.partial(kernel, ny, nx, nz, slots), out_shape=(j...  46.1 us
    unnamed x15, local copies, waits for them, and re-layouts  1.25 us

profile of v3, /device:TPU:8, one launch (start us, length us, event | category | flops | bytes accessed | tf_op | source)
XLA Modules:
  0.0 48.1 jit_solution(3371181222540794235)
XLA Ops:
  0.0 0.0 copy-start
  0.0 0.0 copy-start.1
  0.0 0.0 copy-start.3
  0.0 0.0 copy-start.5
  0.0 46.1 %shard_map.75 = (bf16[4,1024]{1,0:T(4,128)(2,1)S(1)}, f32[1,1]{1,0:T(1,128)}) custom-call(bf16[512,1024]{1,0:T(8,128)(2,1)} %a_hbm.1, bf16[1024,128]{1,0:T(8,128)(2,1)} %w_hbm.1, s32[1,256]{1,0:T(1,128)} %bitcast.15, s32[1,512]{1,0:T(1,128)} %bitcast.11, f32[1,256]{1,0:T(1,128)} %bitcast.17, f32[1,512]{1,0:T(1,128)} %bitcast.13, s32[1,2]{1,0:T(1,128)} %bitcast.19), custom_call_target="tpu_custom_call" | custom-call | flops 268435456 | bytes 1310720 | tf_op jit(solution)/shard_map/pallas_call | solution.py:366
  46.8 0.0 copy-start.2
  46.8 0.0 copy-start.4
  46.8 0.0 copy-start.6
  46.8 0.0 copy-done
  46.8 0.0 copy-done.1
  46.8 0.0 copy-done.3
  46.8 0.0 copy-done.5
  46.9 0.6 %copy-done.2 = s32[512]{0:T(512)S(1)} copy-done((s32[512]{0:T(512)S(1)}, s32[512]{0:T(512)}, u32[]{:S(2)}) %copy-start.2) | copy-done | bytes 2072
  47.5 0.0 copy-done.4
  47.5 0.0 copy-done.6
  47.5 0.6 %copy.13 = bf16[4,1024]{1,0:T(4,128)(2,1)} copy(bf16[4,1024]{1,0:T(4,128)(2,1)S(1)} %get-tuple-element.35) | data formatting | bytes 16384
  (1 shorter events, 0.0 us)
Async XLA Ops:
  0.0 46.8 %copy-start = (bf16[512,1024]{1,0:T(8,128)(2,1)S(1)}, bf16[512,1024]{1,0:T(8,128)(2,1)}, u32[]{:S(2)}) copy-start(bf16[512,1024]{1,0:T(8,128)(2,1)} %a_hbm.1) | copy-start | bytes 3145732
  0.0 46.8 %copy-start.1 = (bf16[1024,128]{1,0:T(8,128)(2,1)S(1)}, bf16[1024,128]{1,0:T(8,128)(2,1)}, u32[]{:S(2)}) copy-start(bf16[1024,128]{1,0:T(8,128)(2,1)} %w_hbm.1) | copy-start | bytes 786436
  0.0 46.8 %copy-start.3 = (f32[512]{0:T(512)S(1)}, f32[512]{0:T(512)}, u32[]{:S(2)}) copy-start(f32[512]{0:T(512)} %param.14) | copy-start | bytes 6148
  0.0 46.8 %copy-start.5 = (f32[256]{0:T(256)S(1)}, f32[256]{0:T(256)}, u32[]{:S(2)}) copy-start(f32[256]{0:T(256)} %param.13) | copy-start | bytes 3076
  46.8 0.7 %copy-start.2 = (s32[512]{0:T(512)S(1)}, s32[512]{0:T(512)}, u32[]{:S(2)}) copy-start(s32[512]{0:T(512)} %param.12) | copy-start | bytes 6148
  46.8 0.7 %copy-start.4 = (s32[256]{0:T(256)S(1)}, s32[256]{0:T(256)}, u32[]{:S(2)}) copy-start(s32[256]{0:T(256)} %param.11) | copy-start | bytes 3076
  46.8 0.7 %copy-start.6 = (s32[2]{0:T(128)S(1)}, s32[2]{0:T(128)}, u32[]{:S(2)}) copy-start(s32[2]{0:T(128)} %param.15) | copy-start | bytes 28

commit v4 on v3

--- a/solution.py
+++ b/solution.py
@@ -29,10 +29,10 @@
 
 def kernel(
     ny, nx, nz, slots, a_hbm, w_hbm, occ_hbm, virt_hbm, occ_en_hbm, virt_en_hbm, slab_hbm,
-    out_ref, most_ref,
-    a_ref, w_ref, occ_s, virt_s, occ_en_s, virt_en_s, slab_s, occ_v, virt_v, occ_en_v,
-    gath, part, core_out, core_in, acc, x_in, z_out, z_in, irrep_ref, slot_ref, energy_ref, place_ref,
-    in_sem, y_send, y_recv, core_send, core_recv, x_send, x_recv, z_send, z_recv, known_sem,
+    out_ref, most_ref, occ_v, virt_v, occ_en_v, virt_en_v, slab_v,
+    a_ref, w_ref, occ_s, virt_s, occ_en_s, virt_en_s, slab_s,
+    gath, part, xc_out, xc_in, z_out, z_in, irrep_ref, slot_ref, energy_ref, place_ref,
+    in_sem, y_send, y_recv, xc_send, xc_recv, z_send, z_recv, known_sem,
 ):
     me_y = lax.axis_index("pair")
     me_c = lax.axis_index("contr")
@@ -63,12 +63,12 @@
         return at(me_x, lax.rem(me_z + step, nz), core)
 
     def near(count, *steps):
-        return sorted({step % count for most in steps for step in (most, -most)} - {0})
+        return sorted({step % count for most in steps for step in (most, -most)} - {0}, key=lambda step: -min(step, count - step))
 
     barrier = pltpu.get_barrier_semaphore()
     greeted = [(lax.rem(me_y + step, ny), me_c) for step in near(ny, 1, 2)]
     greeted += [(me_y, other)]
-    greeted += [(me_y, x_peer(step)) for step in near(nx, 1, 2)]
+    greeted += [(me_y, at(lax.rem(me_x + p, nx), me_z, k)) for p in near(nx, 1, 2) for k in (core, 1 - core)]
     greeted += [(me_y, z_peer(step)) for step in near(nz, 1, 2)]
     for device in greeted:
         pl.semaphore_signal(barrier, inc=1, device_id=device, device_id_type=MESH)
@@ -87,6 +87,8 @@
                 (occ_en_hbm, occ_en_s),
                 (virt_en_hbm, virt_en_s),
                 (occ_en_hbm, occ_en_v),
+                (virt_en_hbm, virt_en_v),
+                (slab_hbm, slab_v),
             ]
         )
     ]
@@ -175,9 +177,10 @@
                 h = turn if sign == 1 else 1 - turn
                 y_copy(sign * dst % ny, sign * dst % ny, h, 1).wait_recv()
 
-    for turn in range(2):
-        send_y(0, 2, turn)
-        send_y(0, 1, turn)
+    send_y(0, 2, 0)
+    send_y(0, 2, 1)
+    send_y(0, 1, 0)
+    send_y(0, 1, 1)
     relay(0)
 
     def mask_amplitudes():
@@ -208,47 +211,35 @@
             total = product if total is None else total + product
         for t in range(width // 128):
             part[group, t] = total[:, t * 128 : (t + 1) * 128]
-        return send_core(group)
+        return send_xc(group)
 
     def strided(group, x, i, k):
         first = (x * nz * CORES + k) * mine + i
         at_rows = pl.ds(first, nz, stride=CORES * mine)
         return jnp.concatenate([part[group, t, at_rows, :] for t in range(width // 128)], axis=1)
 
-    def send_core(group):
+    def send_xc(group):
         for x in range(nx):
-            for i in range(mine):
-                core_out[group, x, i * nz : (i + 1) * nz] = strided(group, x, i, 1 - core)
-        copy = pltpu.make_async_remote_copy(
-            src_ref=core_out.at[group],
-            dst_ref=core_in.at[group],
-            send_sem=core_send.at[group],
-            recv_sem=core_recv.at[group],
-            device_id=(me_y, other),
-            device_id_type=MESH,
-        )
-        copy.start()
-        for x in range(nx):
-            for i in range(mine):
-                acc[group, x, i * nz : (i + 1) * nz] = strided(group, x, i, core)
-        return copy
-
-    def send_x(group, copy):
-        copy.wait_recv()
-        acc[group] = acc[group] + core_in[group]
+            for k in range(CORES):
+                for i in range(mine):
+                    rows_i = strided(group, x, i, k).astype(xc_out.dtype)
+                    xc_out[group, x * CORES + k, i * nz : (i + 1) * nz] = rows_i
         copies = []
-        for step in sorted(range(1, nx), key=lambda step: -min(step, nx - step)):
-            copies.append(
-                pltpu.make_async_remote_copy(
-                    src_ref=acc.at[group, lax.rem(me_x + step, nx)],
-                    dst_ref=x_in.at[group, step - 1],
-                    send_sem=x_send.at[group, step - 1],
-                    recv_sem=x_recv.at[group, step - 1],
-                    device_id=(me_y, x_peer(step)),
-                    device_id_type=MESH,
-                )
-            )
-            copies[-1].start()
+        for p in sorted(range(nx), key=lambda step: -min(step, nx - step)):
+            for q in range(CORES):
+                if p or q:
+                    x, k = lax.rem(me_x + p, nx), lax.rem(core + q, CORES)
+                    copies.append(
+                        pltpu.make_async_remote_copy(
+                            src_ref=xc_out.at[group, x * CORES + k],
+                            dst_ref=xc_in.at[group, p * CORES + q - 1],
+                            send_sem=xc_send.at[group, p * CORES + q - 1],
+                            recv_sem=xc_recv.at[group, p * CORES + q - 1],
+                            device_id=(me_y, at(x, me_z, k)),
+                            device_id_type=MESH,
+                        )
+                    )
+                    copies[-1].start()
         return copies
 
     def z_copy(group, step):
@@ -262,11 +253,11 @@
         )
 
     def send_z(group, copies):
-        total = acc[group, me_x]
+        total = jnp.concatenate([strided(group, me_x, i, core) for i in range(mine)], axis=0)
         for copy in copies:
             copy.wait_recv()
-        for step in range(nx - 1):
-            total = total + x_in[group, step]
+        for step in range(nx * CORES - 1):
+            total = total + xc_in[group, step].astype(jnp.float32)
         for i in range(mine):
             z_out[group, :, i, :] = total[i * nz : (i + 1) * nz]
 
@@ -324,32 +315,29 @@
         row_irrep = jnp.where(row_at == i, jnp.bitwise_xor(occ_s[0, row_occ], virt_s[0, a]), row_irrep)
         row_energy = jnp.where(row_at == i, occ_en_s[0, row_occ] - virt_en_s[0, a], row_energy)
 
-    arrived(1, (0,))
-    send_y(1, 3, 0)
     arrived(2, (0,))
     send_y(2, 4, 0)
-    arrived(1, (1,))
-    send_y(1, 3, 1)
+    send_y(2, 3, 0)
+    arrived(2, (1,))
+    send_y(2, 3, 1)
     relayed(0)
     relay(1)
-    arrived(2, (1,))
-    core_first = multiply(0)
+    arrived(1)
+    x_first = multiply(0)
     relayed(1)
-    x_first = send_x(0, core_first)
     arrived(3)
     arrived(4, (0,))
-    core_second = multiply(1)
+    x_second = multiply(1)
     z_first = send_z(0, x_first)
-    x_second = send_x(1, core_second)
     z_second = send_z(1, x_second)
     finish(0, z_first)
     finish(1, z_second)
 
-    for copy in y_copies + [core_first, core_second] + x_first + x_second + z_first + z_second:
+    for copy in y_copies + x_first + x_second + z_first + z_second:
         copy.wait_send()
 
 
-def contract(amplitudes, integrals, occ_irrep, virt_irrep, occ_energy, virt_energy, slab_start, slots, collective_id=0):
+def contract(amplitudes, integrals, *small, slots, collective_id=0):
     ny = lax.axis_size("pair")
     nx = NX
     nz = lax.axis_size("contr") // (nx * CORES)
@@ -357,7 +345,6 @@
     cols = integrals.shape[1]
     mine = rows // (nx * nz * CORES)
     width = ny // 2 * slots
-    smem = pl.BlockSpec(memory_space=pltpu.SMEM)
     vmem = pl.BlockSpec(memory_space=pltpu.VMEM)
     hbm = pl.BlockSpec(memory_space=pltpu.HBM)
     f32 = jnp.float32
@@ -368,39 +355,29 @@
         out_shape=(
             jax.ShapeDtypeStruct((mine, cols * ny), bf16),
             jax.ShapeDtypeStruct((1, 1), f32),
+            *(jax.ShapeDtypeStruct(array.shape, array.dtype) for array in small),
         ),
         in_specs=[hbm] * 7,
-        out_specs=(vmem, smem),
+        out_specs=(vmem, pl.BlockSpec(memory_space=pltpu.SMEM)) + (vmem,) * 5,
         scratch_shapes=[
             pltpu.VMEM((rows, depth), bf16),
             pltpu.VMEM((depth, cols), bf16),
-            pltpu.SMEM((1, occ_irrep.shape[0]), jnp.int32),
-            pltpu.SMEM((1, virt_irrep.shape[0]), jnp.int32),
-            pltpu.SMEM((1, occ_irrep.shape[0]), f32),
-            pltpu.SMEM((1, virt_irrep.shape[0]), f32),
-            pltpu.SMEM((1, slab_start.shape[0]), jnp.int32),
-            pltpu.VMEM((1, occ_irrep.shape[0]), jnp.int32),
-            pltpu.VMEM((1, virt_irrep.shape[0]), jnp.int32),
-            pltpu.VMEM((1, occ_irrep.shape[0]), f32),
+            *(pltpu.SMEM(array.shape, array.dtype) for array in small),
             pltpu.VMEM((ny, 2, slots, depth // 2), bf16),
             pltpu.VMEM((2, width // 128, rows, 128), f32),
-            pltpu.VMEM((2, nx, mine * nz, width), f32),
-            pltpu.VMEM((2, nx, mine * nz, width), f32),
-            pltpu.VMEM((2, nx, mine * nz, width), f32),
-            pltpu.VMEM((2, nx - 1, mine * nz, width), f32),
+            pltpu.VMEM((2, nx * CORES, mine * nz, width), f32),
+            pltpu.VMEM((2, nx * CORES - 1, mine * nz, width), f32),
             pltpu.VMEM((2, nz, mine, width), f32),
             pltpu.VMEM((2, nz - 1, mine, width), f32),
             pltpu.VMEM((ny, cols), jnp.int32),
             pltpu.VMEM((ny, cols), jnp.int32),
             pltpu.VMEM((ny, cols), f32),
             pltpu.VMEM((2, width, ny // 2 * cols), bf16),
-            dma((10,)),
+            dma((12,)),
             dma((2 * ny,)),
             dma((2 * ny,)),
-            dma((2,)),
-            dma((2,)),
-            dma((2, nx - 1)),
-            dma((2, nx - 1)),
+            dma((2, nx * CORES - 1)),
+            dma((2, nx * CORES - 1)),
             dma((2, nz - 1)),
             dma((2, nz - 1)),
             pltpu.SemaphoreType.REGULAR((2,)),
@@ -411,22 +388,15 @@
         cost_estimate=pl.CostEstimate(
             flops=2 * rows * depth * width * 2, bytes_accessed=2 * depth * (rows + cols), transcendentals=0
         ),
-    )(
-        amplitudes,
-        integrals,
-        occ_irrep[None, :],
-        virt_irrep[None, :],
-        occ_energy[None, :],
-        virt_energy[None, :],
-        slab_start[None, :],
-    )
-
-
-def body(*args):
-    update, most = contract(*args, slots=SLOTS, collective_id=0)
+    )(amplitudes, integrals, *small)
+
+
+def body(amplitudes, integrals, *small):
+    small = [array[None, :] for array in small]
+    update, most, *small = contract(amplitudes, integrals, *small, slots=SLOTS, collective_id=0)
     return lax.cond(
         most[0, 0] > SLOTS - 1,
-        lambda: contract(*args, slots=args[1].shape[1], collective_id=1)[0],
+        lambda: contract(amplitudes, integrals, *small, slots=integrals.shape[1], collective_id=1)[0],
         lambda: update,
     )
 

time: 48.2 us -> 45.3 us (0.940)
  the two profiles are of different devices: /device:TPU:8 before, /device:TPU:1 now
where the time goes in v4:
time: 45.3 us; the launch traced here: 45.2 us
  Pallas kernels  44 us (97%)
  local copies, waits for them, and re-layouts  0.61 us (1%)
  between operations  0.59 us (1%)
    pallas_call x1, Pallas kernels, contract(): pl.pallas_call(functools.partial(kernel, ny, nx, nz, slots), out_shape=(j...  44 us

profile of v4, /device:TPU:1, one launch (start us, length us, event | category | flops | bytes accessed | tf_op | source)
XLA Modules:
  0.0 45.2 jit_solution(6945269503616312410)
XLA Ops:
  0.0 0.0 copy-start
  0.0 0.0 copy-start.1
  0.0 44.0 %shard_map.75 = (bf16[4,1024]{1,0:T(4,128)(2,1)S(1)}, f32[1,1]{1,0:T(1,128)}, s32[1,256]{1,0:T(1,128)S(1)}, s32[1,512]{1,0:T(1,128)S(1)}, f32[1,256]{1,0:T(1,128...) custom-call(bf16[512,1024]{1,0:T(8,128)(2,1)} %a_hbm.1, bf16[1024,128]{1,0:T(8,128)(2,1)} %w_hbm.1, s32[1,256]{1,0:T(1,128)} %bitcast.8, ...), custom_call_target="tpu_custom_call" | custom-call | flops 268435456 | bytes 1310720 | tf_op jit(solution)/shard_map/pallas_call | solution.py:353
  44.5 0.0 copy-done
  44.6 0.0 copy-done.1
  44.6 0.6 %copy.13 = bf16[4,1024]{1,0:T(4,128)(2,1)} copy(bf16[4,1024]{1,0:T(4,128)(2,1)S(1)} %get-tuple-element.45) | data formatting | bytes 16384
  (1 shorter events, 0.0 us)
Async XLA Ops:
  0.0 44.5 %copy-start = (bf16[512,1024]{1,0:T(8,128)(2,1)S(1)}, bf16[512,1024]{1,0:T(8,128)(2,1)}, u32[]{:S(2)}) copy-start(bf16[512,1024]{1,0:T(8,128)(2,1)} %a_hbm.1) | copy-start | bytes 3145732
  0.0 44.5 %copy-start.1 = (bf16[1024,128]{1,0:T(8,128)(2,1)S(1)}, bf16[1024,128]{1,0:T(8,128)(2,1)}, u32[]{:S(2)}) copy-start(bf16[1024,128]{1,0:T(8,128)(2,1)} %w_hbm.1) | copy-start | bytes 786436

commit v5 on v4

--- a/solution.py
+++ b/solution.py
@@ -29,8 +29,8 @@
 
 def kernel(
     ny, nx, nz, slots, a_hbm, w_hbm, occ_hbm, virt_hbm, occ_en_hbm, virt_en_hbm, slab_hbm,
-    out_ref, most_ref, occ_v, virt_v, occ_en_v, virt_en_v, slab_v,
-    a_ref, w_ref, occ_s, virt_s, occ_en_s, virt_en_s, slab_s,
+    out_ref, most_hbm, occ_v, virt_v, occ_en_v, virt_en_v, slab_v,
+    most_ref, a_ref, w_ref, occ_s, virt_s, occ_en_s, virt_en_s, slab_s,
     gath, part, xc_out, xc_in, z_out, z_in, irrep_ref, slot_ref, energy_ref, place_ref,
     in_sem, y_send, y_recv, xc_send, xc_recv, z_send, z_recv, known_sem,
 ):
@@ -50,6 +50,7 @@
     mine = rows // (nx * nz * CORES)
     position = {d: p for p, d in enumerate(ring_order(ny))}
     width = ny // 2 * slots
+    rows_x = rows // nx
 
     def at(x, z, k):
         return (x * nz + z) * CORES + k
@@ -68,20 +69,18 @@
     barrier = pltpu.get_barrier_semaphore()
     greeted = [(lax.rem(me_y + step, ny), me_c) for step in near(ny, 1, 2)]
     greeted += [(me_y, other)]
-    greeted += [(me_y, at(lax.rem(me_x + p, nx), me_z, k)) for p in near(nx, 1, 2) for k in (core, 1 - core)]
-    greeted += [(me_y, z_peer(step)) for step in near(nz, 1, 2)]
-    for device in greeted:
-        pl.semaphore_signal(barrier, inc=1, device_id=device, device_id_type=MESH)
+    greeted += [(me_y, x_peer(step)) for step in near(nx, 1)]
+    greeted += [(me_y, z_peer(step)) for step in near(nz, 1)]
 
     copies_in = [
         pltpu.make_async_copy(src, dst, in_sem.at[i])
         for i, (src, dst) in enumerate(
             [
-                (occ_hbm, occ_s),
-                (virt_hbm, virt_s),
-                (slab_hbm, slab_s),
                 (occ_hbm, occ_v),
                 (virt_hbm, virt_v),
+                (slab_hbm, slab_s),
+                (virt_hbm, virt_s),
+                (occ_hbm, occ_s),
                 (w_hbm, w_ref),
                 (a_hbm, a_ref),
                 (occ_en_hbm, occ_en_s),
@@ -94,55 +93,48 @@
     ]
     for copy in copies_in:
         copy.start()
-    copy_w, copy_a = copies_in[5:7]
-
-    relays = []
-    reach = 2
+    copy_a = copies_in[6]
+
+    for device in greeted:
+        pl.semaphore_signal(barrier, inc=1, device_id=device, device_id_type=MESH)
+
+    relays = [[x_peer(step) for step in near(nx, 1)], [other]]
+    reach, level = 1, 0
     while 2 * reach <= nz // 2:
-        relays.append(reach)
-        reach *= 2
+        relays += [[]] * (level == len(relays))
+        relays[level] = relays[level] + [z_peer(step) for step in near(nz, reach)]
+        reach, level = 2 * reach, level + 1
+    last = len(relays) - 1
 
     def relay(level):
-        if level < len(relays):
-            for step in near(nz, relays[level]):
-                pl.semaphore_signal(
-                    known_sem.at[level], inc=1, device_id=(me_y, z_peer(step)), device_id_type=MESH
-                )
+        for peer in relays[level]:
+            pl.semaphore_signal(known_sem.at[level], inc=1, device_id=(me_y, peer), device_id_type=MESH)
 
     def relayed(level):
-        if level < len(relays):
-            pl.semaphore_wait(known_sem.at[level], len(near(nz, relays[level])))
-
-    spread = jnp.where(iota((occ_count, cols), 0) % occ_pair == iota((occ_count, cols), 1) // slab_second, 1.0, 0.0)
-    own_row = iota((ny, occ_count), 1) // occ_pair == iota((ny, occ_count), 0)
+        pl.semaphore_wait(known_sem.at[level], len(relays[level]))
+
+    own_spread = jnp.where(
+        iota((occ_count, cols), 0) == me_y * occ_pair + iota((occ_count, cols), 1) // slab_second, 1.0, 0.0
+    )
+    before = jnp.where(iota((cols, cols), 0) < iota((cols, cols), 1), 1.0, 0.0)
     b_at = iota((1, cols), 1) % slab_second
-    for copy in copies_in[:5]:
+    for copy in copies_in[:6]:
         copy.wait()
     b_irrep = jnp.zeros((1, cols), jnp.int32)
     for b in range(slab_second):
         b_irrep = jnp.where(b_at == b, virt_s[0, slab_s[0, 1] + b], b_irrep)
-    occ_row = occ_v[...]
-    col_occ = jnp.dot(jnp.where(own_row, occ_row.astype(jnp.float32), 0.0), spread, preferred_element_type=jnp.float32)
-    col_irrep = jnp.bitwise_xor(col_occ.astype(jnp.int32), b_irrep)
-    before = jnp.where(iota((cols, cols), 0) < iota((cols, cols), 1), 1.0, 0.0)
-    hot = jnp.concatenate([jnp.where(col_irrep == g, 1.0, 0.0) for g in range(IRREPS)], axis=0)
-    counted = jnp.dot(hot, before, preferred_element_type=jnp.float32)
-    slot = jnp.zeros((ny, cols), jnp.float32)
-    for g in range(IRREPS):
-        slot = jnp.where(col_irrep == g, counted[g * ny : (g + 1) * ny], slot)
-    most_ref[0, 0] = jnp.max(slot)
-    slot = slot.astype(jnp.int32)
-    irrep_ref[...] = col_irrep
-    slot_ref[...] = slot
-
+    occ_row = occ_v[...].astype(jnp.float32)
+    own_occ = jnp.dot(occ_row, own_spread, preferred_element_type=jnp.float32)
+    own_irrep = jnp.bitwise_xor(own_occ.astype(jnp.int32), b_irrep)
+    own_hot = jnp.where(own_irrep == iota((IRREPS, cols), 0), 1.0, 0.0)
+    own_counted = jnp.dot(own_hot, before, preferred_element_type=jnp.float32)
+    own_slot = jnp.sum(own_hot * own_counted, axis=0, keepdims=True).astype(jnp.int32)
     local_occ = depth // virt_count
     kc_irrep = jnp.concatenate(
         [jnp.bitwise_xor(virt_v[...], occ_s[0, me_c * local_occ + k]) for k in range(local_occ)], axis=1
     )
-
-    key = irrep_ref[pl.ds(me_y, 1), :] * slots + slot_ref[pl.ds(me_y, 1), :]
+    key = own_irrep * slots + own_slot
     pick = jnp.where(iota((IRREPS * slots, cols), 0) == key, 1.0, 0.0).astype(jnp.bfloat16)
-    copy_w.wait()
     picked = lax.dot_general(pick, w_ref[...], NT, preferred_element_type=jnp.float32)
     kept = picked[:slots]
     for g in range(1, IRREPS):
@@ -200,38 +192,33 @@
 
         lax.fori_loop(0, occ_pair, mask, 0)
 
+    def far_first(count):
+        return sorted(range(count), key=lambda step: -min(step, count - step))
+
     def multiply(group):
         first = group * ny // 2
-        total = None
-        for h in range(2):
-            block = gath[first : first + ny // 2, h].reshape(width, half)
-            product = lax.dot_general(
-                a_ref[:, h * half : (h + 1) * half], block, NT, preferred_element_type=jnp.float32
+        blocks = [gath[first : first + ny // 2, h].reshape(width, half) for h in range(2)]
+        copies = []
+        for p in far_first(nx):
+            x = lax.rem(me_x + p, nx)
+            at_rows = pl.ds(pl.multiple_of(x * rows_x, rows_x), rows_x)
+            total = sum(
+                lax.dot_general(
+                    a_ref[at_rows, h * half : (h + 1) * half], blocks[h], NT, preferred_element_type=jnp.float32
+                )
+                for h in range(2)
             )
-            total = product if total is None else total + product
-        for t in range(width // 128):
-            part[group, t] = total[:, t * 128 : (t + 1) * 128]
-        return send_xc(group)
-
-    def strided(group, x, i, k):
-        first = (x * nz * CORES + k) * mine + i
-        at_rows = pl.ds(first, nz, stride=CORES * mine)
-        return jnp.concatenate([part[group, t, at_rows, :] for t in range(width // 128)], axis=1)
-
-    def send_xc(group):
-        for x in range(nx):
+            for t in range(width // 128):
+                part[group, p, t] = total[:, t * 128 : (t + 1) * 128]
             for k in range(CORES):
                 for i in range(mine):
-                    rows_i = strided(group, x, i, k).astype(xc_out.dtype)
-                    xc_out[group, x * CORES + k, i * nz : (i + 1) * nz] = rows_i
-        copies = []
-        for p in sorted(range(nx), key=lambda step: -min(step, nx - step)):
+                    xc_out[group, p * CORES + k, i * nz : (i + 1) * nz] = strided(group, p, i, k)
             for q in range(CORES):
                 if p or q:
-                    x, k = lax.rem(me_x + p, nx), lax.rem(core + q, CORES)
+                    k = lax.rem(core + q, CORES)
                     copies.append(
                         pltpu.make_async_remote_copy(
-                            src_ref=xc_out.at[group, x * CORES + k],
+                            src_ref=xc_out.at[group, p * CORES + k],
                             dst_ref=xc_in.at[group, p * CORES + q - 1],
                             send_sem=xc_send.at[group, p * CORES + q - 1],
                             recv_sem=xc_recv.at[group, p * CORES + q - 1],
@@ -242,6 +229,10 @@
                     copies[-1].start()
         return copies
 
+    def strided(group, p, i, k):
+        at_rows = pl.ds(k * mine + i, nz, stride=CORES * mine)
+        return jnp.concatenate([part[group, p, t, at_rows, :] for t in range(width // 128)], axis=1)
+
     def z_copy(group, step):
         return pltpu.make_async_remote_copy(
             src_ref=z_out.at[group, lax.rem(me_z + step, nz)],
@@ -253,7 +244,7 @@
         )
 
     def send_z(group, copies):
-        total = jnp.concatenate([strided(group, me_x, i, core) for i in range(mine)], axis=0)
+        total = xc_out[group, core]
         for copy in copies:
             copy.wait_recv()
         for step in range(nx * CORES - 1):
@@ -276,9 +267,9 @@
         rest = total - high.astype(jnp.float32)
         middle = rest.astype(jnp.bfloat16)
         low = (rest - middle.astype(jnp.float32)).astype(jnp.bfloat16)
-        placed = sum(
-            jnp.dot(term, place_ref[group], preferred_element_type=jnp.float32) for term in (low, middle, high)
-        )
+        terms = jnp.concatenate([term.astype(jnp.float32) for term in (low, middle, high)], axis=0).astype(jnp.bfloat16)
+        placed = jnp.dot(terms, place_ref[group], preferred_element_type=jnp.float32)
+        placed = placed[:mine] + placed[mine : 2 * mine] + placed[2 * mine :]
         blocks = group_blocks(group)
         for p, block in enumerate(blocks):
             value = placed[:, p * cols : (p + 1) * cols]
@@ -290,6 +281,21 @@
         return [lax.rem(me_y + d, ny) for d in ring_order(ny)[group * ny // 2 : (group + 1) * ny // 2]]
 
     mask_amplitudes()
+
+    spread = jnp.where(iota((occ_count, cols), 0) % occ_pair == iota((occ_count, cols), 1) // slab_second, 1.0, 0.0)
+    own_row = iota((ny, occ_count), 1) // occ_pair == iota((ny, occ_count), 0)
+    col_occ = jnp.dot(jnp.where(own_row, occ_row, 0.0), spread, preferred_element_type=jnp.float32)
+    col_irrep = jnp.bitwise_xor(col_occ.astype(jnp.int32), b_irrep)
+    hot = jnp.concatenate([jnp.where(col_irrep == g, 1.0, 0.0) for g in range(IRREPS)], axis=0)
+    counted = jnp.dot(hot, before, preferred_element_type=jnp.float32)
+    slot = jnp.zeros((ny, cols), jnp.float32)
+    for g in range(IRREPS):
+        slot = jnp.where(col_irrep == g, counted[g * ny : (g + 1) * ny], slot)
+    most_ref[0, 0] = jnp.max(slot)
+    copy_most = pltpu.make_async_copy(most_ref, most_hbm, in_sem.at[len(copies_in)])
+    copy_most.start()
+    irrep_ref[...] = col_irrep
+    slot_ref[...] = slot.astype(jnp.int32)
 
     seat = iota((width, cols), 0)
     for group in range(2):
@@ -315,26 +321,30 @@
         row_irrep = jnp.where(row_at == i, jnp.bitwise_xor(occ_s[0, row_occ], virt_s[0, a]), row_irrep)
         row_energy = jnp.where(row_at == i, occ_en_s[0, row_occ] - virt_en_s[0, a], row_energy)
 
+    relayed(0)
+    relay(1)
     arrived(2, (0,))
     send_y(2, 4, 0)
     send_y(2, 3, 0)
     arrived(2, (1,))
     send_y(2, 3, 1)
-    relayed(0)
-    relay(1)
     arrived(1)
+    relayed(1)
+    if last > 1:
+        relay(2)
     x_first = multiply(0)
-    relayed(1)
     arrived(3)
     arrived(4, (0,))
     x_second = multiply(1)
+    if last > 1:
+        relayed(2)
     z_first = send_z(0, x_first)
     z_second = send_z(1, x_second)
     finish(0, z_first)
-    finish(1, z_second)
-
+    copy_most.wait()
     for copy in y_copies + x_first + x_second + z_first + z_second:
         copy.wait_send()
+    finish(1, z_second)
 
 
 def contract(amplitudes, integrals, *small, slots, collective_id=0):
@@ -358,13 +368,14 @@
             *(jax.ShapeDtypeStruct(array.shape, array.dtype) for array in small),
         ),
         in_specs=[hbm] * 7,
-        out_specs=(vmem, pl.BlockSpec(memory_space=pltpu.SMEM)) + (vmem,) * 5,
+        out_specs=(vmem, hbm) + (vmem,) * 5,
         scratch_shapes=[
+            pltpu.SMEM((1, 1), f32),
             pltpu.VMEM((rows, depth), bf16),
             pltpu.VMEM((depth, cols), bf16),
             *(pltpu.SMEM(array.shape, array.dtype) for array in small),
             pltpu.VMEM((ny, 2, slots, depth // 2), bf16),
-            pltpu.VMEM((2, width // 128, rows, 128), f32),
+            pltpu.VMEM((2, nx, width // 128, rows // nx, 128), f32),
             pltpu.VMEM((2, nx * CORES, mine * nz, width), f32),
             pltpu.VMEM((2, nx * CORES - 1, mine * nz, width), f32),
             pltpu.VMEM((2, nz, mine, width), f32),
@@ -373,14 +384,14 @@
             pltpu.VMEM((ny, cols), jnp.int32),
             pltpu.VMEM((ny, cols), f32),
             pltpu.VMEM((2, width, ny // 2 * cols), bf16),
-            dma((12,)),
+            dma((13,)),
             dma((2 * ny,)),
             dma((2 * ny,)),
             dma((2, nx * CORES - 1)),
             dma((2, nx * CORES - 1)),
             dma((2, nz - 1)),
             dma((2, nz - 1)),
-            pltpu.SemaphoreType.REGULAR((2,)),
+            pltpu.SemaphoreType.REGULAR((3,)),
         ],
         compiler_params=pltpu.CompilerParams(
             collective_id=collective_id, has_side_effects=True, vmem_limit_bytes=60 * 1024 * 1024

time: 45.3 us -> 43.9 us (0.969)
  Pallas kernels: 44 us -> 42.5 us
    pallas_call x1, Pallas kernels: 44 us -> 42.5 us  [contract(): pl.pallas_call(functools.partial(kernel, ny, nx, nz, slots), out_shape=(j...]
where the time goes in v5:
time: 43.9 us; the launch traced here: 43.7 us
  Pallas kernels  42.5 us (97%)
  local copies, waits for them, and re-layouts  0.61 us (1%)
  between operations  0.59 us (1%)
    pallas_call x1, Pallas kernels, contract(): pl.pallas_call(functools.partial(kernel, ny, nx, nz, slots), out_shape=(j...  42.5 us

profile of v5, /device:TPU:1, one launch (start us, length us, event | category | flops | bytes accessed | tf_op | source)
XLA Modules:
  0.0 43.7 jit_solution(13761841519729234753)
XLA Ops:
  0.0 0.0 copy-start
  0.0 0.0 copy-start.1
  0.0 42.5 %shard_map.75 = (bf16[4,1024]{1,0:T(4,128)(2,1)S(1)}, f32[1,1]{1,0:T(1,128)}, s32[1,256]{1,0:T(1,128)S(1)}, s32[1,512]{1,0:T(1,128)S(1)}, f32[1,256]{1,0:T(1,128...) custom-call(bf16[512,1024]{1,0:T(8,128)(2,1)} %a_hbm.1, bf16[1024,128]{1,0:T(8,128)(2,1)} %w_hbm.1, s32[1,256]{1,0:T(1,128)} %bitcast.8, ...), custom_call_target="tpu_custom_call" | custom-call | flops 268435456 | bytes 1310720 | tf_op jit(solution)/shard_map/pallas_call | solution.py:363
  43.1 0.0 copy-done
  43.1 0.0 copy-done.1
  43.1 0.6 %copy.13 = bf16[4,1024]{1,0:T(4,128)(2,1)} copy(bf16[4,1024]{1,0:T(4,128)(2,1)S(1)} %get-tuple-element.45) | data formatting | bytes 16384
  (1 shorter events, 0.0 us)
Async XLA Ops:
  0.0 43.1 %copy-start = (bf16[512,1024]{1,0:T(8,128)(2,1)S(1)}, bf16[512,1024]{1,0:T(8,128)(2,1)}, u32[]{:S(2)}) copy-start(bf16[512,1024]{1,0:T(8,128)(2,1)} %a_hbm.1) | copy-start | bytes 3145732
  0.0 43.1 %copy-start.1 = (bf16[1024,128]{1,0:T(8,128)(2,1)S(1)}, bf16[1024,128]{1,0:T(8,128)(2,1)}, u32[]{:S(2)}) copy-start(bf16[1024,128]{1,0:T(8,128)(2,1)} %w_hbm.1) | copy-start | bytes 786436

commit v6 on v5

--- a/solution.py
+++ b/solution.py
@@ -169,10 +169,22 @@
                 h = turn if sign == 1 else 1 - turn
                 y_copy(sign * dst % ny, sign * dst % ny, h, 1).wait_recv()
 
+    def whole_copy(sign):
+        return pltpu.make_async_remote_copy(
+            src_ref=gath.at[position[0]],
+            dst_ref=gath.at[position[sign % ny]],
+            send_sem=y_send.at[2 * (sign % ny)],
+            recv_sem=y_recv.at[2 * (sign % ny)],
+            device_id=(lax.rem(me_y - sign % ny + ny, ny), me_c),
+            device_id_type=MESH,
+        )
+
     send_y(0, 2, 0)
     send_y(0, 2, 1)
-    send_y(0, 1, 0)
-    send_y(0, 1, 1)
+    whole_copies = [whole_copy(sign) for sign in (1, -1)]
+    for copy in whole_copies:
+        copy.start()
+    y_copies += whole_copies
     relay(0)
 
     def mask_amplitudes():
@@ -282,6 +294,20 @@
 
     mask_amplitudes()
 
+    relayed(0)
+    relay(1)
+    arrived(2, (0,))
+    send_y(2, 4, 0)
+    send_y(2, 3, 0)
+    arrived(2, (1,))
+    send_y(2, 3, 1)
+    for copy in whole_copies:
+        copy.wait_recv()
+    relayed(1)
+    if last > 1:
+        relay(2)
+    x_first = multiply(0)
+
     spread = jnp.where(iota((occ_count, cols), 0) % occ_pair == iota((occ_count, cols), 1) // slab_second, 1.0, 0.0)
     own_row = iota((ny, occ_count), 1) // occ_pair == iota((ny, occ_count), 0)
     col_occ = jnp.dot(jnp.where(own_row, occ_row, 0.0), spread, preferred_element_type=jnp.float32)
@@ -321,18 +347,6 @@
         row_irrep = jnp.where(row_at == i, jnp.bitwise_xor(occ_s[0, row_occ], virt_s[0, a]), row_irrep)
         row_energy = jnp.where(row_at == i, occ_en_s[0, row_occ] - virt_en_s[0, a], row_energy)
 
-    relayed(0)
-    relay(1)
-    arrived(2, (0,))
-    send_y(2, 4, 0)
-    send_y(2, 3, 0)
-    arrived(2, (1,))
-    send_y(2, 3, 1)
-    arrived(1)
-    relayed(1)
-    if last > 1:
-        relay(2)
-    x_first = multiply(0)
     arrived(3)
     arrived(4, (0,))
     x_second = multiply(1)

time: 43.9 us -> 43.9 us (level)
  no operation moved by 1% of the time
where the time goes in v6:
time: 43.9 us; the launch traced here: 43.7 us
  Pallas kernels  42.5 us (97%)
  local copies, waits for them, and re-layouts  0.61 us (1%)
  between operations  0.59 us (1%)
    pallas_call x1, Pallas kernels, contract(): pl.pallas_call(functools.partial(kernel, ny, nx, nz, slots), out_shape=(j...  42.5 us

profile of v6, /device:TPU:1, one launch (start us, length us, event | category | flops | bytes accessed | tf_op | source)
XLA Modules:
  0.0 43.7 jit_solution(11783476623641133592)
XLA Ops:
  0.0 0.0 copy-start
  0.0 0.0 copy-start.1
  0.0 42.5 %shard_map.75 = (bf16[4,1024]{1,0:T(4,128)(2,1)S(1)}, f32[1,1]{1,0:T(1,128)}, s32[1,256]{1,0:T(1,128)S(1)}, s32[1,512]{1,0:T(1,128)S(1)}, f32[1,256]{1,0:T(1,128...) custom-call(bf16[512,1024]{1,0:T(8,128)(2,1)} %a_hbm.1, bf16[1024,128]{1,0:T(8,128)(2,1)} %w_hbm.1, s32[1,256]{1,0:T(1,128)} %bitcast.8, ...), custom_call_target="tpu_custom_call" | custom-call | flops 268435456 | bytes 1310720 | tf_op jit(solution)/shard_map/pallas_call | solution.py:377
  43.1 0.0 copy-done
  43.1 0.0 copy-done.1
  43.1 0.6 %copy.13 = bf16[4,1024]{1,0:T(4,128)(2,1)} copy(bf16[4,1024]{1,0:T(4,128)(2,1)S(1)} %get-tuple-element.45) | data formatting | bytes 16384
  (1 shorter events, 0.0 us)
Async XLA Ops:
  0.0 43.1 %copy-start = (bf16[512,1024]{1,0:T(8,128)(2,1)S(1)}, bf16[512,1024]{1,0:T(8,128)(2,1)}, u32[]{:S(2)}) copy-start(bf16[512,1024]{1,0:T(8,128)(2,1)} %a_hbm.1) | copy-start | bytes 3145732
  0.0 43.1 %copy-start.1 = (bf16[1024,128]{1,0:T(8,128)(2,1)S(1)}, bf16[1024,128]{1,0:T(8,128)(2,1)}, u32[]{:S(2)}) copy-start(bf16[1024,128]{1,0:T(8,128)(2,1)} %w_hbm.1) | copy-start | bytes 786436
